TPU v7x, 32 devices: a whole 2x2x4 slice. The times are simulated.
32 devices in a mesh: groups: 2 (over y), date: 4 (over z), pix: 2 (over x), chan: 2 (over core).
Axes of the slice: x: 2, y: 2, z: 4, core: 2. Of those that a mesh axis runs over, the one named last changes fastest.
Arguments:
- frames: bfloat16 [128, 4, 64, 128], P(('groups', 'date'), 'pix'), parts along dimension 0, may hold values from -6 to 6
- spatial_weight: bfloat16 [3, 3, 64, 64], P(None, None, None, 'chan'), may hold values from -0.25 to 0.25
- spatial_bias: float32 [64], P('chan'), may hold values from -3 to 3
- temporal_weight: bfloat16 [64, 64, 16], P('date', 'chan'), may hold values from -0.1875 to 0.1875
- temporal_bias: float32 [16], replicated, may hold values from -4 to 4
- head_weight: float32 [16], replicated, may hold values from -3 to 3
- labels: int32 [8, 128], P(('groups', 'pix'), ('date', 'chan')), parts along dimension 0, may hold values 0 or 1
Outputs:
- logits: float32 [8, 128], P(('groups', 'pix'), ('date', 'chan')), parts along dimension 0
- grad_spatial: float32 [6, 3, 64, 64], P('groups', None, None, 'chan'), parts along dimension 0
- grad_temporal: float32 [64, 64, 32], P('date', 'chan', 'groups'), parts along dimension 2
There are 2 independent parts, one for each index of `groups`. A program takes and returns all parts, laid end to end along the dimension named above; an argument that names none is the same for every part. Nothing has to cross between parts.
All inputs are finite; a program needn't handle non-finite values. No bound on the sum of `labels` on one device may be relied on, other than what follows from the above.
Results may differ from a plain program's by a relative error of at most 0.024.
Values may be sent and summed in bfloat16 or wider, within the bound.
A program may use at most 64 MiB of HBM per device.

v0:
```python
import jax
import jax.numpy as jnp
from jax import lax
from jax.sharding import PartitionSpec as P


def with_halo(block, sides, width):
    for axis, dim in sides:
        count = lax.axis_size(axis)
        forward = [(i, i + 1) for i in range(count - 1)]
        backward = [(target, source) for source, target in forward]
        low = lax.ppermute(
            lax.slice_in_dim(block, block.shape[dim] - width, None, axis=dim), axis, forward
        )
        high = lax.ppermute(lax.slice_in_dim(block, 0, width, axis=dim), axis, backward)
        block = jnp.concatenate([low, block, high], axis=dim)
    return block


def shards(
    frames, spatial_weight, spatial_bias, temporal_weight, temporal_bias, head_weight, labels
):
    dates_here, rows, channels, columns = frames.shape
    padded = with_halo(frames, (("pix", 1),), 1)
    padded = jnp.pad(padded, ((0, 0), (0, 0), (0, 0), (1, 1)))
    preact = spatial_bias[None, None, :, None]
    for row_off in range(3):
        for col_off in range(3):
            window = padded[:, row_off : row_off + rows, :, col_off : col_off + columns]
            preact = preact + jnp.einsum(
                "ticj,co->tioj",
                window,
                spatial_weight[row_off, col_off],
                preferred_element_type=jnp.float32,
            )
    sigmoid_pre = jax.nn.sigmoid(preact)
    hidden = (preact * sigmoid_pre).astype(jnp.bfloat16)
    partial_feat = jnp.einsum(
        "tioj,tof->fij", hidden, temporal_weight, preferred_element_type=jnp.float32
    )
    feature = (
        lax.psum_scatter(partial_feat, ("date", "chan"), scatter_dimension=2, tiled=True)
        + temporal_bias[:, None, None]
    )
    sigmoid_feat = jax.nn.sigmoid(feature)
    logits = jnp.einsum("fij,f->ij", feature * sigmoid_feat, head_weight)
    dlogit = jax.nn.sigmoid(logits) - labels.astype(jnp.float32)
    feature_grad = (
        dlogit[None]
        * head_weight[:, None, None]
        * sigmoid_feat
        * (1.0 + feature * (1.0 - sigmoid_feat))
    ).astype(jnp.bfloat16)
    full_grad = lax.all_gather(feature_grad, ("date", "chan"), axis=2, tiled=True)
    temporal_part = jnp.einsum(
        "tioj,fij->tof", hidden, full_grad, preferred_element_type=jnp.float32
    )
    hidden_grad = jnp.einsum(
        "fij,tof->tioj", full_grad, temporal_weight, preferred_element_type=jnp.float32
    )
    preact_grad = (hidden_grad * sigmoid_pre * (1.0 + preact * (1.0 - sigmoid_pre))).astype(
        jnp.bfloat16
    )
    rows_out = []
    for row_off in range(3):
        cols_out = []
        for col_off in range(3):
            window = padded[:, row_off : row_off + rows, :, col_off : col_off + columns]
            cols_out.append(
                jnp.einsum("ticj,tioj->co", window, preact_grad, preferred_element_type=jnp.float32)
            )
        rows_out.append(jnp.stack(cols_out))
    spatial_part = jnp.stack(rows_out)
    grad_temporal = lax.psum(temporal_part, "pix")
    grad_spatial = lax.psum(spatial_part, ("date", "pix"))
    return (logits, grad_spatial, grad_temporal)


def solution(mesh):
    placed = (
        P(("groups", "date"), "pix", None, None),
        P(None, None, None, "chan"),
        P("chan"),
        P("date", "chan", None),
        P(),
        P(),
        P(("groups", "pix"), ("date", "chan")),
    )
    return jax.shard_map(
        shards,
        mesh=mesh,
        in_specs=placed,
        out_specs=(
            P(("groups", "pix"), ("date", "chan")),
            P("groups", None, None, "chan"),
            P("date", "chan", "groups"),
        ),
        check_vma=False,
    )
```

profile of v0, /device:TPU:0, one launch (start us, length us, event | category | flops | bytes accessed | tf_op | source)
XLA Modules:
  0.0 157.4 jit_solution(17748076628413484052)
XLA Ops:
  7.2 1.1 fusion.79
  8.4 4.9 %collective-permute-start = (bf16[16,1,64,128]{3,2,1,0:T(8,128)(2,1)S(1)}, bf16[16,1,64,128]{3,2,1,0:T(8,128)(2,1)S(1)}, u32[]{:S(2)}, u32[]{:S(2)}) collective-permute-start(bf16[16,1,64,128]{3,2,1,0:T(8,128)(2,1)S(1)} %get-tuple-element.11), channel_id=1, source_target_pairs={{0,2},{1,3},{4,6},{5,7},{8,10},{9,11},{12,14},{13,15},{16,18},{17,... | collective-permute-start | bytes 786440 | tf_op jit(solution)/shard_map/ppermute | solution.py:12
  13.3 1.4 collective-permute-start.1
  14.7 1.3 fusion.47
  16.0 2.8 %collective-permute-done = bf16[16,1,64,128]{3,2,1,0:T(8,128)(2,1)S(1)} collective-permute-done((bf16[16,1,64,128]{3,2,1,0:T(8,128)(2,1)S(1)}, bf16[16,1,64,128]{3,2,1,0:T(8,128)(2,1)S(1)}, u32[]{:S(2)}, u32[]{:S(2)}) %collective-permute-start) | collective-permute-done | bytes 262176 | tf_op jit(solution)/shard_map/ppermute | solution.py:12
  18.8 4.3 %collective-permute-done.1 = bf16[16,1,64,128]{3,2,1,0:T(8,128)(2,1)S(1)} collective-permute-done((bf16[16,1,64,128]{3,2,1,0:T(8,128)(2,1)S(1)}, bf16[16,1,64,128]{3,2,1,0:T(8,128)(2,1)S(1)}, u32[]{:S(2)}, u32[]{:S(2)}) %collective-permute-start.1) | collective-permute-done | bytes 262176 | tf_op jit(solution)/shard_map/ppermute | solution.py:15
  23.0 1.1 fusion.5
  24.2 0.4 fusion.40
  24.5 0.4 fusion.51
  26.0 0.2 fusion.15
  26.2 1.2 multiply_convert_fusion
  27.6 0.8 copy.76
  28.4 1.7 %reshape.35 = f32[128,32]{1,0:T(8,128)} reshape(f32[128,2,16]{2,1,0:T(2,128)} %bitcast.179) | data formatting | bytes 32768
  30.2 2.2 %fusion.78 = (bf16[16,2,64,128]{3,2,1,0:T(8,128)(2,1)}, bf16[16,2,64,128]{3,2,1,0:T(8,128)(2,1)}, bf16[16,2,64,128]{3,2,1,0:T(8,128)(2,1)}, bf16[16,2,64,128]{3,...) fusion(bf16[16,4,64,130]{3,2,1,0:T(8,128)(2,1)S(1)} %fusion.5), kind=kLoop, calls=%fused_computation.104 | loop fusion | bytes 6291456 | tf_op jit(solution)/shard_map/slice | solution.py:29
  32.4 28.2 %reduce-scatter.4.cloned.1.call-done = f32[16,32]{1,0:T(8,128)} async-done(((f32[128,32]{1,0:T(8,128)}), f32[16,32]{1,0:T(8,128)}) %reduce-scatter.4.cloned.1.call-update) | async-done | bytes 2064
  60.6 0.8 reshape.36
  61.9 14.0 %all_gather.3 = bf16[16,2,128]{0,1,2:T(2,128)(2,1)S(1)} all-gather(bf16[16,2,16]{0,1,2:T(2,128)(2,1)S(1)} %copy.31), channel_id=1, replica_groups=mesh['groups'=2,'date'=4,'pix'=2,'chan'=2] {'date','chan'}, dimensions={2}, use_global_device_ids=true | all-gather | bytes 9216 | tf_op jit(solution)/shard_map/all_gather | solution.py:54
  75.9 1.4 fusion.16
  77.3 0.3 convolution_bitcast_fusion.10
  77.6 0.3 convolution_bitcast_fusion.4
  77.9 0.3 convolution_bitcast_fusion.7
  78.4 0.3 convolution_bitcast_fusion.11
  78.6 0.3 convolution_bitcast_fusion.5
  78.9 0.3 convolution_bitcast_fusion.6
  79.2 0.3 convolution_bitcast_fusion.8
  79.4 0.3 convolution_bitcast_fusion.9
  79.8 0.3 convolution_bitcast_fusion.3
  80.1 0.7 pad_maximum_fusion.2
  80.8 0.3 convolution_bitcast_fusion.1
  81.0 10.8 %psum.15 = f32[16,32,16]{1,2,0:T(8,128)} all-reduce(f32[16,32,16]{1,2,0:T(8,128)S(1)} %convolution_bitcast_fusion.1), channel_id=1, replica_groups=mesh['groups'=2,'date'=4,'pix'=2,'chan'=2] {'pix'}, use_global_device_ids=true, to_apply=%region_2.3 | all-reduce | flops 8192 | bytes 65536 | tf_op jit(solution)/shard_map/psum | solution.py:74
  91.8 57.2 %all-reduce.3.cloned.1.call-done = f32[3,3,64,32]{2,3,1,0:T(8,128)} async-done(((f32[3,3,64,32]{2,3,1,0:T(8,128)}), f32[3,3,64,32]{2,3,1,0:T(8,128)}) %all-reduce.3.cloned.1.call-update) | async-done | bytes 73744 | tf_op jit(solution)/shard_map/psum | solution.py:75
  149.0 1.6 %copy.115 = f32[3,3,64,32]{2,3,1,0:T(8,128)} copy(f32[3,3,64,32]{2,3,1,0:T(8,128)} %all-reduce.3.cloned.1.call-done) | data formatting | bytes 147456
  (50 shorter events, 2.3 us)
Async XLA Ops:
  7.2 20.3 %copy-start = (bf16[16,32,16]{1,2,0:T(8,128)(2,1)S(1)}, bf16[16,32,16]{1,2,0:T(8,128)(2,1)}, u32[]{:S(2)}) copy-start(bf16[16,32,16]{1,2,0:T(8,128)(2,1)} %param.10) | copy-start | bytes 49156
  7.2 15.9 %copy-start.1 = (bf16[16,2,64,128]{3,2,1,0:T(8,128)(2,1)S(1)}, bf16[16,2,64,128]{3,2,1,0:T(8,128)(2,1)}, u32[]{:S(2)}) copy-start(bf16[16,2,64,128]{3,2,1,0:T(8,128)(2,1)} %param.7) | copy-start | bytes 1572868
  7.2 53.4 %reduce-scatter.4.cloned.1.call-start = ((), (), s32[]{:S(2)}) async-start(), calls=%async_computation.2 | async-start | bytes 73728
  8.4 10.4 %collective-permute-start = (bf16[16,1,64,128]{3,2,1,0:T(8,128)(2,1)S(1)}, bf16[16,1,64,128]{3,2,1,0:T(8,128)(2,1)S(1)}, u32[]{:S(2)}, u32[]{:S(2)}) collective-permute-start(bf16[16,1,64,128]{3,2,1,0:T(8,128)(2,1)S(1)} %get-tuple-element.11), channel_id=1, source_target_pairs={{0,2},{1,3},{4,6},{5,7},{8,10},{9,11},{12,14},{13,15},{16,18},{17,... | collective-permute-start | bytes 786440 | tf_op jit(solution)/shard_map/ppermute | solution.py:12
  13.2 10.9 %copy-start.10 = (bf16[3,3,64,32]{2,3,1,0:T(8,128)(2,1)S(1)}, bf16[3,3,64,32]{2,3,1,0:T(8,128)(2,1)}, u32[]{:S(2)}) copy-start(bf16[3,3,64,32]{2,3,1,0:T(8,128)(2,1)} %param.8) | copy-start | bytes 110596
  13.3 9.8 %collective-permute-start.1 = (bf16[16,1,64,128]{3,2,1,0:T(8,128)(2,1)S(1)}, bf16[16,1,64,128]{3,2,1,0:T(8,128)(2,1)S(1)}, u32[]{:S(2)}, u32[]{:S(2)}) collective-permute-start(bf16[16,1,64,128]{3,2,1,0:T(8,128)(2,1)S(1)} %get-tuple-element.12), channel_id=1, source_target_pairs={{2,0},{3,1},{6,4},{7,5},{10,8},{11,9},{14,12},{15,13},{18,16},{19,... | collective-permute-start | bytes 786440 | tf_op jit(solution)/shard_map/ppermute | solution.py:15
  25.3 0.7 copy-start.15
  25.4 0.8 copy-start.2
  30.1 31.4 %copy-start.13 = (f32[16]{0:T(128)S(1)}, f32[16]{0:T(128)}, u32[]{:S(2)}) copy-start(f32[16]{0:T(128)} %param.11) | copy-start | bytes 196
  30.1 31.4 %copy-start.14 = (f32[16]{0:T(128)S(1)}, f32[16]{0:T(128)}, u32[]{:S(2)}) copy-start(f32[16]{0:T(128)} %param.12) | copy-start | bytes 196
  30.1 31.5 %copy-start.11 = (s32[2,16]{1,0:T(2,128)S(1)}, s32[2,16]{1,0:T(2,128)}, u32[]{:S(2)}) copy-start(s32[2,16]{1,0:T(2,128)} %param.13) | copy-start | bytes 388
  30.1 118.9 %all-reduce.3.cloned.1.call-start = ((), (), s32[]{:S(2)}) async-start(), calls=%async_computation.1 | async-start | bytes 294912 | tf_op jit(solution)/shard_map/psum | solution.py:75
  32.4 44.9 %copy-start.3 = (bf16[16,2,64,128]{3,2,1,0:T(8,128)(2,1)S(1)}, bf16[16,2,64,128]{3,2,1,0:T(8,128)(2,1)}, u32[]{:S(2)}) copy-start(bf16[16,2,64,128]{3,2,1,0:T(8,128)(2,1)} %copy-done.2) | copy-start | bytes 1572868
  61.6 16.2 %copy-start.12 = (f32[1,2,16]{2,0,1:T(1,128)}, f32[1,2,16]{2,0,1:T(1,128)S(1)}, u32[]{:S(2)}) copy-start(f32[1,2,16]{2,0,1:T(1,128)S(1)} %fusion.28) | copy-start | bytes 388
  77.3 1.0 copy-start.9
  77.3 1.3 copy-start.8
  77.6 1.3 copy-start.7
  77.9 1.3 copy-start.6
  78.1 1.3 copy-start.5
  78.6 1.2 copy-start.4
Sparse Core Ops, SparseCore 0:
  30.2 30.3 reduce-scatter.3
  80.9 68.0 all-reduce.2
where the time goes:
time: 158 us; the launch traced here: 157 us
  waiting for transfers between devices  92.5 us (59%)
  blocking collectives  24.7 us (16%)
  between operations  14.3 us (9%)
  local copies, waits for them, and re-layouts  8.89 us (6%)
  matrix products  8.7 us (6%)
  starting transfers between devices  6.36 us (4%)
  other arithmetic  1.98 us (1%)
    psum x1, waiting for transfers between devices, shards(): grad_spatial = lax.psum(spatial_part, ('date', 'pix'))  57.2 us
    unnamed x3, waiting for transfers between devices  28.2 us
    all_gather x1, blocking collectives, shards(): lax.all_gather(feature_grad, ('date', 'chan'), axis=2, tiled=True)  14 us
    psum x1, blocking collectives, shards(): grad_temporal = lax.psum(temporal_part, 'pix')  10.8 us
    unnamed x37, local copies, waits for them, and re-layouts  5.36 us
    ppermute x1, starting transfers between devices, with_halo(): lax.ppermute(lax.slice_in_dim(block, block.shape[dim] - width, None, axis...  4.86 us
    ppermute x1, waiting for transfers between devices, with_halo(): lax.ppermute(lax.slice_in_dim(block, 0, width, axis=dim), axis, backward)  4.27 us
    dot_general x9, matrix products, shards(): jnp.einsum('ticj,co->tioj', window, spatial_weight[row_off, col_off], pre...  4.27 us
  transfers between devices with their start and end apart: 4, of which 4 were waited for; matrix products, arithmetic and copies ran while one was open for 2% of the time, Pallas kernels for 0%

commit v1 on v0

--- a/solution.py
+++ b/solution.py
@@ -72,7 +72,8 @@
         rows_out.append(jnp.stack(cols_out))
     spatial_part = jnp.stack(rows_out)
     grad_temporal = lax.psum(temporal_part, "pix")
-    grad_spatial = lax.psum(spatial_part, ("date", "pix"))
+    parts = lax.all_gather(spatial_part, ("date", "pix"))
+    grad_spatial = jnp.sum(parts, axis=0)
     return (logits, grad_spatial, grad_temporal)
 
 

time: 158 us -> 132 us (0.84)
  waiting for transfers between devices: 92.5 us -> 35.3 us
  blocking collectives: 24.7 us -> 57.3 us
  local copies, waits for them, and re-layouts: 8.89 us -> 7.05 us
    psum x1 -> x0, waiting for transfers between devices: 57.2 us -> none  [shards(): grad_spatial = lax.psum(spatial_part, ('date', 'pix'))]
    all_gather x0 -> x1, blocking collectives: none -> 33 us  [shards(): parts = lax.all_gather(spatial_part, ('date', 'pix'))]
    unnamed x37 -> x36, local copies, waits for them, and re-layouts: 5.36 us -> 3.5 us
    unnamed x3 -> x2, waiting for transfers between devices: 28.2 us -> 28.2 us
  transfers between devices with their start and end apart: 4 -> 3, of which waited for: 4 -> 3; matrix products, arithmetic and copies ran while one was open for 2% -> 3% of each run, Pallas kernels for 0% -> 0%
where the time goes in v1:
time: 132 us; the launch traced here: 131 us
  blocking collectives  57.3 us (43%)
  waiting for transfers between devices  35.3 us (27%)
  between operations  14.3 us (11%)
  matrix products  8.79 us (7%)
  local copies, waits for them, and re-layouts  7.05 us (5%)
  starting transfers between devices  6.32 us (5%)
  other arithmetic  2.12 us (2%)
    all_gather x1, blocking collectives, shards(): parts = lax.all_gather(spatial_part, ('date', 'pix'))  33 us
    unnamed x2, waiting for transfers between devices  28.2 us
    all_gather x1, blocking collectives, shards(): lax.all_gather(feature_grad, ('date', 'chan'), axis=2, tiled=True)  14 us
    psum x1, blocking collectives, shards(): grad_temporal = lax.psum(temporal_part, 'pix')  10.3 us
    ppermute x1, starting transfers between devices, with_halo(): lax.ppermute(lax.slice_in_dim(block, block.shape[dim] - width, None, axis...  4.86 us
    dot_general x9, matrix products, shards(): jnp.einsum('ticj,co->tioj', window, spatial_weight[row_off, col_off], pre...  4.31 us
    ppermute x1, waiting for transfers between devices, with_halo(): lax.ppermute(lax.slice_in_dim(block, 0, width, axis=dim), axis, backward)  4.27 us
    unnamed x36, local copies, waits for them, and re-layouts  3.5 us
  transfers between devices with their start and end apart: 3, of which 3 were waited for; matrix products, arithmetic and copies ran while one was open for 3% of the time, Pallas kernels for 0%

profile of v1, /device:TPU:0, one launch (start us, length us, event | category | flops | bytes accessed | tf_op | source)
XLA Modules:
  0.0 131.1 jit_solution(15926971236711038668)
XLA Ops:
  7.2 1.1 fusion.79
  8.4 4.9 %collective-permute-start = (bf16[16,1,64,128]{3,2,1,0:T(8,128)(2,1)S(1)}, bf16[16,1,64,128]{3,2,1,0:T(8,128)(2,1)S(1)}, u32[]{:S(2)}, u32[]{:S(2)}) collective-permute-start(bf16[16,1,64,128]{3,2,1,0:T(8,128)(2,1)S(1)} %get-tuple-element.11), channel_id=1, source_target_pairs={{0,2},{1,3},{4,6},{5,7},{8,10},{9,11},{12,14},{13,15},{16,18},{17,... | collective-permute-start | bytes 786440 | tf_op jit(solution)/shard_map/ppermute | solution.py:12
  13.3 1.4 %collective-permute-start.1 = (bf16[16,1,64,128]{3,2,1,0:T(8,128)(2,1)S(1)}, bf16[16,1,64,128]{3,2,1,0:T(8,128)(2,1)S(1)}, u32[]{:S(2)}, u32[]{:S(2)}) collective-permute-start(bf16[16,1,64,128]{3,2,1,0:T(8,128)(2,1)S(1)} %get-tuple-element.12), channel_id=1, source_target_pairs={{2,0},{3,1},{6,4},{7,5},{10,8},{11,9},{14,12},{15,13},{18,16},{19,... | collective-permute-start | bytes 786440 | tf_op jit(solution)/shard_map/ppermute | solution.py:15
  14.7 1.3 fusion.47
  16.0 2.8 %collective-permute-done = bf16[16,1,64,128]{3,2,1,0:T(8,128)(2,1)S(1)} collective-permute-done((bf16[16,1,64,128]{3,2,1,0:T(8,128)(2,1)S(1)}, bf16[16,1,64,128]{3,2,1,0:T(8,128)(2,1)S(1)}, u32[]{:S(2)}, u32[]{:S(2)}) %collective-permute-start) | collective-permute-done | bytes 262176 | tf_op jit(solution)/shard_map/ppermute | solution.py:12
  18.8 4.3 %collective-permute-done.1 = bf16[16,1,64,128]{3,2,1,0:T(8,128)(2,1)S(1)} collective-permute-done((bf16[16,1,64,128]{3,2,1,0:T(8,128)(2,1)S(1)}, bf16[16,1,64,128]{3,2,1,0:T(8,128)(2,1)S(1)}, u32[]{:S(2)}, u32[]{:S(2)}) %collective-permute-start.1) | collective-permute-done | bytes 262176 | tf_op jit(solution)/shard_map/ppermute | solution.py:15
  23.0 1.1 fusion.5
  24.2 0.4 fusion.40
  24.5 0.4 fusion.51
  25.6 0.2 fusion.42
  26.0 0.3 fusion.15
  26.2 1.2 multiply_convert_fusion
  27.6 0.8 copy.76
  28.4 1.7 %reshape.36 = f32[128,32]{1,0:T(8,128)} reshape(f32[128,2,16]{2,1,0:T(2,128)} %bitcast.181) | data formatting | bytes 32768
  30.2 2.3 %fusion.78 = (bf16[16,2,64,128]{3,2,1,0:T(8,128)(2,1)}, bf16[16,2,64,128]{3,2,1,0:T(8,128)(2,1)}, bf16[16,2,64,128]{3,2,1,0:T(8,128)(2,1)}, bf16[16,2,64,128]{3,...) fusion(bf16[16,4,64,130]{3,2,1,0:T(8,128)(2,1)S(1)} %fusion.5), kind=kLoop, calls=%fused_computation.104 | loop fusion | bytes 6291456 | tf_op jit(solution)/shard_map/slice | solution.py:29
  32.4 28.2 %reduce-scatter.4.cloned.1.call-done = f32[16,32]{1,0:T(8,128)} async-done(((f32[128,32]{1,0:T(8,128)}), f32[16,32]{1,0:T(8,128)}) %reduce-scatter.4.cloned.1.call-update) | async-done | bytes 2064
  60.6 0.8 reshape.37
  61.9 14.0 %all_gather.9 = bf16[16,2,128]{0,1,2:T(2,128)(2,1)S(1)} all-gather(bf16[16,2,16]{0,1,2:T(2,128)(2,1)S(1)} %copy.31), channel_id=1, replica_groups=mesh['groups'=2,'date'=4,'pix'=2,'chan'=2] {'date','chan'}, dimensions={2}, use_global_device_ids=true | all-gather | bytes 9216 | tf_op jit(solution)/shard_map/all_gather | solution.py:54
  75.9 1.4 %fusion.16 = bf16[16,2,32,128]{3,2,1,0:T(8,128)(2,1)S(1)} fusion(f32[16,2,32,128]{3,2,1,0:T(8,128)} %get-tuple-element.14, bf16[16,32,16]{1,2,0:T(8,128)(2,1)S(1)} %copy-done, bf16[16,2,128]{2,0,1:T(8,128)(2,1)S(1)} %copy.32), kind=kOutput, calls=%fused_computation.21 | convolution fusion | flops 5373952 | bytes 811008 | tf_op jit(solution)/shard_map/fij,tof->tioj/dot_general | solution.py:58
  77.4 0.3 convolution_bitcast_fusion.10
  77.6 0.3 convolution_bitcast_fusion.4
  77.9 0.3 convolution_bitcast_fusion.1
  78.2 0.3 convolution_bitcast_fusion.7
  78.5 10.3 %psum.7 = f32[16,32,16]{1,2,0:T(8,128)} all-reduce(f32[16,32,16]{1,2,0:T(8,128)S(1)} %convolution_bitcast_fusion.1), channel_id=1, replica_groups=mesh['groups'=2,'date'=4,'pix'=2,'chan'=2] {'pix'}, use_global_device_ids=true, to_apply=%region_2.3 | all-reduce | flops 8192 | bytes 65536 | tf_op jit(solution)/shard_map/psum | solution.py:74
  88.8 0.3 convolution_bitcast_fusion.11
  89.1 0.3 convolution_bitcast_fusion.5
  89.3 0.3 convolution_bitcast_fusion.6
  89.6 0.3 convolution_bitcast_fusion.8
  89.9 0.3 convolution_bitcast_fusion.9
  90.2 0.3 convolution_bitcast_fusion.3
  90.5 33.0 %all-gather = f32[24,3,64,32]{2,3,1,0:T(8,128)S(1)} all-gather(f32[3,3,64,32]{2,3,1,0:T(8,128)S(1)} %pad_maximum_fusion.2), channel_id=2, replica_groups=mesh['groups'=2,'date'=4,'pix'=2,'chan'=2] {'date','pix'}, dimensions={0}, use_global_device_ids=true | all-gather | bytes 663552 | tf_op jit(solution)/shard_map/all_gather | solution.py:75
  123.5 0.8 reduce_sum.9
  (48 shorter events, 1.8 us)
Async XLA Ops:
  7.2 20.3 %copy-start = (bf16[16,32,16]{1,2,0:T(8,128)(2,1)S(1)}, bf16[16,32,16]{1,2,0:T(8,128)(2,1)}, u32[]{:S(2)}) copy-start(bf16[16,32,16]{1,2,0:T(8,128)(2,1)} %param.10) | copy-start | bytes 49156
  7.2 15.9 %copy-start.1 = (bf16[16,2,64,128]{3,2,1,0:T(8,128)(2,1)S(1)}, bf16[16,2,64,128]{3,2,1,0:T(8,128)(2,1)}, u32[]{:S(2)}) copy-start(bf16[16,2,64,128]{3,2,1,0:T(8,128)(2,1)} %param.7) | copy-start | bytes 1572868
  7.2 53.4 %reduce-scatter.4.cloned.1.call-start = ((), (), s32[]{:S(2)}) async-start(), calls=%async_computation.1 | async-start | bytes 73728
  8.4 10.4 %collective-permute-start = (bf16[16,1,64,128]{3,2,1,0:T(8,128)(2,1)S(1)}, bf16[16,1,64,128]{3,2,1,0:T(8,128)(2,1)S(1)}, u32[]{:S(2)}, u32[]{:S(2)}) collective-permute-start(bf16[16,1,64,128]{3,2,1,0:T(8,128)(2,1)S(1)} %get-tuple-element.11), channel_id=1, source_target_pairs={{0,2},{1,3},{4,6},{5,7},{8,10},{9,11},{12,14},{13,15},{16,18},{17,... | collective-permute-start | bytes 786440 | tf_op jit(solution)/shard_map/ppermute | solution.py:12
  13.2 10.9 %copy-start.10 = (bf16[3,3,64,32]{2,3,1,0:T(8,128)(2,1)S(1)}, bf16[3,3,64,32]{2,3,1,0:T(8,128)(2,1)}, u32[]{:S(2)}) copy-start(bf16[3,3,64,32]{2,3,1,0:T(8,128)(2,1)} %param.8) | copy-start | bytes 110596
  13.3 9.8 %collective-permute-start.1 = (bf16[16,1,64,128]{3,2,1,0:T(8,128)(2,1)S(1)}, bf16[16,1,64,128]{3,2,1,0:T(8,128)(2,1)S(1)}, u32[]{:S(2)}, u32[]{:S(2)}) collective-permute-start(bf16[16,1,64,128]{3,2,1,0:T(8,128)(2,1)S(1)} %get-tuple-element.12), channel_id=1, source_target_pairs={{2,0},{3,1},{6,4},{7,5},{10,8},{11,9},{14,12},{15,13},{18,16},{19,... | collective-permute-start | bytes 786440 | tf_op jit(solution)/shard_map/ppermute | solution.py:15
  25.3 0.7 copy-start.15
  25.4 0.8 copy-start.2
  30.1 31.4 %copy-start.13 = (f32[16]{0:T(128)S(1)}, f32[16]{0:T(128)}, u32[]{:S(2)}) copy-start(f32[16]{0:T(128)} %param.11) | copy-start | bytes 196
  30.1 31.4 %copy-start.14 = (f32[16]{0:T(128)S(1)}, f32[16]{0:T(128)}, u32[]{:S(2)}) copy-start(f32[16]{0:T(128)} %param.12) | copy-start | bytes 196
  30.1 31.5 %copy-start.11 = (s32[2,16]{1,0:T(2,128)S(1)}, s32[2,16]{1,0:T(2,128)}, u32[]{:S(2)}) copy-start(s32[2,16]{1,0:T(2,128)} %param.13) | copy-start | bytes 388
  32.4 44.9 %copy-start.3 = (bf16[16,2,64,128]{3,2,1,0:T(8,128)(2,1)S(1)}, bf16[16,2,64,128]{3,2,1,0:T(8,128)(2,1)}, u32[]{:S(2)}) copy-start(bf16[16,2,64,128]{3,2,1,0:T(8,128)(2,1)} %copy-done.2) | copy-start | bytes 1572868
  61.7 16.2 %copy-start.12 = (f32[1,2,16]{2,0,1:T(1,128)}, f32[1,2,16]{2,0,1:T(1,128)S(1)}, u32[]{:S(2)}) copy-start(f32[1,2,16]{2,0,1:T(1,128)S(1)} %fusion.28) | copy-start | bytes 388
  77.4 11.4 %copy-start.9 = (bf16[16,2,64,128]{3,2,1,0:T(8,128)(2,1)S(1)}, bf16[16,2,64,128]{3,2,1,0:T(8,128)(2,1)}, u32[]{:S(2)}) copy-start(bf16[16,2,64,128]{3,2,1,0:T(8,128)(2,1)} %get-tuple-element.3) | copy-start | bytes 1572868
  77.4 11.7 %copy-start.8 = (bf16[16,2,64,128]{3,2,1,0:T(8,128)(2,1)S(1)}, bf16[16,2,64,128]{3,2,1,0:T(8,128)(2,1)}, u32[]{:S(2)}) copy-start(bf16[16,2,64,128]{3,2,1,0:T(8,128)(2,1)} %get-tuple-element.4) | copy-start | bytes 1572868
  77.6 11.7 %copy-start.7 = (bf16[16,2,64,128]{3,2,1,0:T(8,128)(2,1)S(1)}, bf16[16,2,64,128]{3,2,1,0:T(8,128)(2,1)}, u32[]{:S(2)}) copy-start(bf16[16,2,64,128]{3,2,1,0:T(8,128)(2,1)} %get-tuple-element.5) | copy-start | bytes 1572868
  78.2 11.4 %copy-start.6 = (bf16[16,2,64,128]{3,2,1,0:T(8,128)(2,1)S(1)}, bf16[16,2,64,128]{3,2,1,0:T(8,128)(2,1)}, u32[]{:S(2)}) copy-start(bf16[16,2,64,128]{3,2,1,0:T(8,128)(2,1)} %get-tuple-element.6) | copy-start | bytes 1572868
  78.5 11.4 %copy-start.5 = (bf16[16,2,64,128]{3,2,1,0:T(8,128)(2,1)S(1)}, bf16[16,2,64,128]{3,2,1,0:T(8,128)(2,1)}, u32[]{:S(2)}) copy-start(bf16[16,2,64,128]{3,2,1,0:T(8,128)(2,1)} %get-tuple-element.7) | copy-start | bytes 1572868
  89.1 1.1 copy-start.4
Sparse Core Ops, SparseCore 0:
  30.2 30.3 reduce-scatter.3
